TPU v7x, 512 devices: a whole 4x8x8 slice. The times are simulated.
512 devices in a mesh: dp: 64 (over x, y, core), tensor: 8 (over z).
Axes of the slice: x: 4, y: 8, z: 8, core: 2. Of those that a mesh axis runs over, the one named last changes fastest.
Arguments:
- features: bfloat16 [32768, 128], P(('dp', 'tensor')), may hold values from -24 to 24
- output_gradient: bfloat16 [32768, 28672], P('dp', 'tensor'), may hold values from -0.03125 to 0.03125
- live_token_count: int32 [64], replicated, may hold values from 1 to 512, 24576 in all
- former_range_lengths: int32 [64], replicated, may hold values from 1792 to 12544, as said below
- target_range_lengths: int32 [63], replicated, may hold values from 1790 to 12659, as said below
- keeper_rank_list: int32 [63], replicated, may hold values from 0 to 63, as said below
- former_master_weight: float32 [8, 802816], P('tensor', 'dp'), may hold values from -6 to 6
- former_first_moment: float32 [8, 802816], P('tensor', 'dp'), may hold values from -6 to 6
- former_second_moment: float32 [8, 802816], P('tensor', 'dp'), may hold values from 0.05 to 4
Outputs:
- new_master: float32 [8, 810176], P('tensor', 'dp')
- new_first: float32 [8, 810176], P('tensor', 'dp')
- new_second: float32 [8, 810176], P('tensor', 'dp')
Inputs may be any that keep to these rules, and one draw needn't show every extreme that they name: `former_range_lengths`: summing to 458752; the boundary after the first k ranges lies within 2688 of k * 7168; the longest range is exactly 12544. `target_range_lengths`: summing to 458752; the boundary after the first k ranges lies between -2688 and 2690 from (k * 458752) // 63; the longest range is exactly 12659. `keeper_rank_list`: Increasing; exactly one data rank is missing.
All inputs are finite; a program needn't handle non-finite values.
Results may differ from a plain program's by a relative error of at most 0.0003.
Values may be sent and summed in bfloat16 or wider, within the bound.
A program may use at most 64 MiB of HBM per device.

v0:
```python
import jax
import jax.numpy as jnp
from jax import lax
from jax.sharding import PartitionSpec as P

BETA_ONE = 0.9
BETA_TWO = 0.95
EPSILON = 1e-08
DECAY = 0.1
LEARN_RATE = 0.02
CORRECT_ONE = 1.0 - 2.6561398887587544e-05
CORRECT_TWO = 1.0 - 0.005920529220333998


def passed_along(value, axis, steps):
    count = lax.axis_size(axis)
    initial, last = (max(0, -steps), min(count, count - steps))
    return lax.ppermute(value, axis, [(source, source + steps) for source in range(initial, last)])


def range_bounds(lengths):
    return jnp.concatenate([jnp.zeros((1,), jnp.int32), jnp.cumsum(lengths)])


def adamw_step(master, moment_one, moment_two, gradient, in_range):
    first_next = BETA_ONE * moment_one + (1.0 - BETA_ONE) * gradient
    second_next = BETA_TWO * moment_two + (1.0 - BETA_TWO) * gradient * gradient
    update = first_next / CORRECT_ONE / (jnp.sqrt(second_next / CORRECT_TWO) + EPSILON)
    master_next = master - LEARN_RATE * (update + DECAY * master)
    return (
        jnp.where(in_range, master_next, jnp.zeros_like(master_next)),
        jnp.where(in_range, first_next, jnp.zeros_like(first_next)),
        jnp.where(in_range, second_next, jnp.zeros_like(second_next)),
    )


def read_range(source, anchor, upper_edge, range_begin, length, width):
    slot_ids = jnp.arange(width, dtype=jnp.int32)
    positions = range_begin + slot_ids
    in_range = (positions >= anchor) & (positions < upper_edge) & (slot_ids < length)
    padded = jnp.pad(source, ((0, 0), (width, width)))
    shifted = lax.dynamic_slice_in_dim(padded, range_begin - anchor + width, width, 1)
    return jnp.where(in_range[None, :], shifted, jnp.zeros_like(shifted))


def move_joint(combined):
    received = {0: combined}
    for offset in (-2, -1, 1, 2):
        received[offset] = passed_along(combined, "dp", -offset)
    return received


def on_device(
    features,
    output_gradient,
    live_token_count,
    former_range_lengths,
    target_range_lengths,
    keeper_rank_list,
    former_master_weight,
    former_first_moment,
    former_second_moment,
):
    data_rank_count = lax.axis_size("dp")
    local_rank = lax.axis_index("dp")
    width_ff = output_gradient.shape[1]
    weight_rows = features.shape[1]
    even_block = weight_rows * width_ff // data_rank_count
    spread = 3 * even_block // 8
    old_cap = former_master_weight.shape[1]
    new_cap = even_block + even_block // (data_rank_count - 1) + 2 * spread + 2
    features_all = lax.all_gather(features, "tensor", axis=0, tiled=True)
    row_total = features_all.shape[0]
    owner_flag = jnp.any(keeper_rank_list == local_rank)
    live_rows = (jnp.arange(row_total, dtype=jnp.int32) < live_token_count[local_rank]) & owner_flag
    masked = jnp.where(live_rows[:, None], features_all, jnp.zeros_like(features_all))
    old_bounds = range_bounds(former_range_lengths)
    new_bounds = range_bounds(target_range_lengths)
    cursor_position = jnp.minimum(
        jnp.sum((keeper_rank_list < local_rank).astype(jnp.int32)), data_rank_count - 2
    )
    range_begin = new_bounds[cursor_position]
    length = jnp.where(owner_flag, target_range_lengths[cursor_position], 0)
    states = jnp.concatenate(
        [former_master_weight, former_first_moment, former_second_moment], axis=0
    )
    gradient = jnp.zeros((new_cap,), jnp.float32)
    partial_grad = lax.dot_general(
        masked, output_gradient, (((0,), (0,)), ((), ())), preferred_element_type=jnp.float32
    )
    block_grad = lax.psum_scatter(
        partial_grad.reshape(even_block * lax.axis_size("dp")),
        "dp",
        scatter_dimension=0,
        tiled=True,
    )
    padded_grad = jnp.pad(block_grad, (0, old_cap - even_block))[None, :]
    joint_parts = move_joint(jnp.concatenate([states, padded_grad], axis=0))
    state_parts = {offset: joint_parts[offset][:3] for offset in joint_parts}
    grad_parts = {offset: joint_parts[offset][3:] for offset in joint_parts}
    for offset in (-2, -1, 0, 1, 2):
        source_rank = local_rank + offset
        inside = (source_rank >= 0) & (source_rank < data_rank_count)
        anchor = jnp.clip(source_rank, 0, data_rank_count - 1) * even_block
        upper_edge = jnp.where(inside, anchor + even_block, anchor)
        gradient = (
            gradient
            + read_range(grad_parts[offset], anchor, upper_edge, range_begin, length, new_cap)[0]
        )
    gathered = jnp.zeros((3, new_cap), jnp.float32)
    for offset in (-2, -1, 0, 1, 2):
        source_rank = local_rank + offset
        inside = (source_rank >= 0) & (source_rank < data_rank_count)
        clipped = jnp.clip(source_rank, 0, data_rank_count - 1)
        anchor = old_bounds[clipped]
        upper_edge = jnp.where(inside, old_bounds[clipped + 1], anchor)
        gathered = gathered + read_range(
            state_parts[offset], anchor, upper_edge, range_begin, length, new_cap
        )
    in_range = jnp.arange(new_cap, dtype=jnp.int32) < length
    master, moment_one, moment_two = adamw_step(
        gathered[0], gathered[1], gathered[2], gradient, in_range
    )
    return (master[None, :], moment_one[None, :], moment_two[None, :])


def solution(mesh):
    placed = (
        P(("dp", "tensor"), None),
        P("dp", "tensor"),
        P(),
        P(),
        P(),
        P(),
        P("tensor", "dp"),
        P("tensor", "dp"),
        P("tensor", "dp"),
    )
    return jax.shard_map(
        on_device,
        mesh=mesh,
        in_specs=placed,
        out_specs=(P("tensor", "dp"), P("tensor", "dp"), P("tensor", "dp")),
        check_vma=False,
    )
```

profile of v0, /device:TPU:1, one launch (start us, length us, event | category | flops | bytes accessed | tf_op | source)
XLA Modules:
  0.0 274.2 jit_solution(12048442376321917097)
XLA Ops:
  7.2 25.9 %all_gather.3 = bf16[512,128]{1,0:T(8,128)(2,1)S(1)} all-gather(bf16[64,128]{1,0:T(8,128)(2,1)} %param.9), channel_id=1, replica_groups=mesh['dp'=64,'tensor'=8] {'tensor'}, dimensions={0}, use_global_device_ids=true | all-gather | bytes 147456 | tf_op jit(solution)/shard_map/all_gather | solution.py:72
  33.1 1.3 compare_reduce_fusion
  34.4 1.2 dynamic_slice.73
  35.7 1.3 fusion.45
  37.0 2.8 %fusion.17 = f32[128,3584]{1,0:T(8,128)S(1)} fusion(bf16[512,3584]{1,0:T(8,128)(2,1)} %param.10, bf16[512,128]{1,0:T(8,128)(2,1)S(1)} %all_gather.3, pred[512]{0:T(512)(128)(4,1)S(1)} %fusion.45), kind=kOutput, calls=%fused_computation.36 | convolution fusion | flops 469827584 | bytes 5636608 | tf_op jit(solution)/shard_map/dot_general | solution.py:88
  39.8 1.3 reshape.195
  41.2 0.6 fusion.46
  42.5 0.1 copy.16
  42.7 0.1 reduce-window.18
  42.7 0.1 reduce
  42.9 0.1 copy.17
  43.0 0.1 reduce-window.19
  43.1 0.1 reduce.1
  43.3 0.6 dynamic_slice.70
  43.9 0.7 fusion.49
  53.4 0.6 dynamic_slice.69
  61.7 1.3 dynamic-slice
  63.6 1.9 fusion.21
  65.5 1.8 fusion.23
  67.3 177.0 %all-reduce.14.cloned.1.call-done = f32[458752]{0:T(1024)} async-done(((f32[458752]{0:T(1024)}), f32[458752]{0:T(1024)}) %all-reduce.14.cloned.1.call-update) | async-done | bytes 1835024
  244.3 0.8 dynamic-slice.1
  245.1 0.2 pad_maximum_fusion
  245.3 2.5 collective-permute-start
  247.8 2.5 collective-permute-start.1
  250.3 2.3 collective-permute-start.2
  252.6 1.3 collective-permute-start.3
  253.9 1.3 fusion.25
  255.2 3.4 %collective-permute-done.2 = f32[4,12544]{1,0:T(4,128)S(1)} collective-permute-done((f32[4,12544]{1,0:T(4,128)S(1)}, f32[4,12544]{1,0:T(4,128)S(1)}, u32[]{:S(2)}, u32[]{:S(2)}) %collective-permute-start.2) | collective-permute-done | bytes 200736 | tf_op jit(solution)/shard_map/ppermute | solution.py:18
  258.6 3.9 %collective-permute-done.3 = f32[4,12544]{1,0:T(4,128)S(1)} collective-permute-done((f32[4,12544]{1,0:T(4,128)S(1)}, f32[4,12544]{1,0:T(4,128)S(1)}, u32[]{:S(2)}, u32[]{:S(2)}) %collective-permute-start.3) | collective-permute-done | bytes 200736 | tf_op jit(solution)/shard_map/ppermute | solution.py:18
  262.5 1.2 fusion.4
  264.0 2.3 fusion.44
  266.3 1.0 fusion.43
  (24 shorter events, 0.5 us)
Async XLA Ops:
  7.2 237.1 %all-reduce.14.cloned.1.call-start = ((), (), s32[]{:S(2)}) async-start(), calls=%async_computation | async-start | bytes 3670016
  39.8 1.4 copy-start.5
  39.8 2.8 %copy-start.4 = (s32[63]{0:T(128)S(1)}, s32[63]{0:T(128)}, u32[]{:S(2)}) copy-start(s32[63]{0:T(128)} %param.13) | copy-start | bytes 760
  39.8 3.1 %copy-start.3 = (s32[64]{0:T(128)S(1)}, s32[64]{0:T(128)}, u32[]{:S(2)}) copy-start(s32[64]{0:T(128)} %param.12) | copy-start | bytes 772
  39.8 205.3 %copy-start = (f32[1,12544]{1,0:T(1,128)S(1)}, f32[1,12544]{1,0:T(1,128)}, u32[]{:S(2)}) copy-start(f32[1,12544]{1,0:T(1,128)} %param.17) | copy-start | bytes 150532
  39.8 205.3 %copy-start.1 = (f32[1,12544]{1,0:T(1,128)S(1)}, f32[1,12544]{1,0:T(1,128)}, u32[]{:S(2)}) copy-start(f32[1,12544]{1,0:T(1,128)} %param.16) | copy-start | bytes 150532
  39.8 205.3 %copy-start.2 = (f32[1,12544]{1,0:T(1,128)S(1)}, f32[1,12544]{1,0:T(1,128)}, u32[]{:S(2)}) copy-start(f32[1,12544]{1,0:T(1,128)} %param.15) | copy-start | bytes 150532
  245.3 9.8 %collective-permute-start = (f32[4,12544]{1,0:T(4,128)S(1)}, f32[4,12544]{1,0:T(4,128)S(1)}, u32[]{:S(2)}, u32[]{:S(2)}) collective-permute-start(f32[4,12544]{1,0:T(4,128)S(1)} %pad_maximum_fusion), channel_id=1, source_target_pairs={{0,16},{8,24},{16,32},{24,40},{32,48},{40,56},{48,64},{56,72},{64,... | collective-permute-start | bytes 602120 | tf_op jit(solution)/shard_map/ppermute | solution.py:18
  247.8 7.4 %collective-permute-start.1 = (f32[4,12544]{1,0:T(4,128)S(1)}, f32[4,12544]{1,0:T(4,128)S(1)}, u32[]{:S(2)}, u32[]{:S(2)}) collective-permute-start(f32[4,12544]{1,0:T(4,128)S(1)} %pad_maximum_fusion), channel_id=1, source_target_pairs={{0,8},{8,16},{16,24},{24,32},{32,40},{40,48},{48,56},{56,64},{64,7... | collective-permute-start | bytes 602120 | tf_op jit(solution)/shard_map/ppermute | solution.py:18
  250.3 8.3 %collective-permute-start.2 = (f32[4,12544]{1,0:T(4,128)S(1)}, f32[4,12544]{1,0:T(4,128)S(1)}, u32[]{:S(2)}, u32[]{:S(2)}) collective-permute-start(f32[4,12544]{1,0:T(4,128)S(1)} %pad_maximum_fusion), channel_id=1, source_target_pairs={{8,0},{16,8},{24,16},{32,24},{40,32},{48,40},{56,48},{64,56},{72,6... | collective-permute-start | bytes 602120 | tf_op jit(solution)/shard_map/ppermute | solution.py:18
  252.6 9.9 %collective-permute-start.3 = (f32[4,12544]{1,0:T(4,128)S(1)}, f32[4,12544]{1,0:T(4,128)S(1)}, u32[]{:S(2)}, u32[]{:S(2)}) collective-permute-start(f32[4,12544]{1,0:T(4,128)S(1)} %pad_maximum_fusion), channel_id=1, source_target_pairs={{16,0},{24,8},{32,16},{40,24},{48,32},{56,40},{64,48},{72,56},{80,... | collective-permute-start | bytes 602120 | tf_op jit(solution)/shard_map/ppermute | solution.py:18
Sparse Core Ops, SparseCore 0:
  41.3 202.9 all-reduce.13
where the time goes:
time: 276 us; the launch traced here: 274 us
  waiting for transfers between devices  184 us (67%)
  between operations  32.1 us (12%)
  blocking collectives  25.9 us (9%)
  other arithmetic  13.4 us (5%)
  starting transfers between devices  8.56 us (3%)
  local copies, waits for them, and re-layouts  6.98 us (3%)
  matrix products  2.81 us (1%)
    unnamed x2, waiting for transfers between devices  177 us
    all_gather x1, blocking collectives, on_device(): features_all = lax.all_gather(features, 'tensor', axis=0, tiled=True)  25.9 us
    ppermute x4, starting transfers between devices, passed_along(): lax.ppermute(value, axis, [(source, source + steps) for source in range(i...  8.52 us
    ppermute x4, waiting for transfers between devices, passed_along(): lax.ppermute(value, axis, [(source, source + steps) for source in range(i...  7.34 us
  transfers between devices with their start and end apart: 5, of which 3 were waited for; matrix products, arithmetic and copies ran while one was open for 3% of the time, Pallas kernels for 0%

commit v1 on v0

v1 whole, which is shorter than its diff:
```python
import functools
import jax
import jax.numpy as jnp
from jax import lax
from jax.experimental import pallas as pl
from jax.experimental.pallas import tpu as pltpu
from jax.sharding import PartitionSpec as P

BETA_ONE = 0.9
BETA_TWO = 0.95
EPSILON = 1e-08
DECAY = 0.1
LEARN_RATE = 0.02
CORRECT_ONE = 1.0 - 2.6561398887587544e-05
CORRECT_TWO = 1.0 - 0.005920529220333998

NX, NY, NC = 4, 8, 2
NDP = NX * NY * NC
NZ = 8
ROWS = 128
COLS = 28
TOK = 512
TOK_Z = TOK // NZ
LANES = 128
BLOCK = 7168
OLD_CAP = 12544
OLD_ROWS = OLD_CAP // LANES
NEW_CAP = 12659
OUT_ROWS = 99
WIN = 104
GRAD_ROWS = 304
SLOTS = 20
FRONT = 2
OFFSETS = (-2, -1, 1, 2)

CHUNKS = ((0, 20, "x"), (20, 8, "y"))


def main_kernel(
    live_in, keeper_in, former_in, target_in, feat, og, st0, st1, st2, states, grad, meta,
    og_v, feat_all, mt, live, keeper, former, target, *rest,
):
    n = len(CHUNKS)
    part, core, r1, r2, fin = (rest[k * n : (k + 1) * n] for k in range(5))
    (ag_s, ag_r, og_sem, st_s, st_r, st_loc, co_s, co_r, s1_s, s1_r, s2_s, s2_r, rd_s, rd_r,
     in_sem) = rest[5 * n :]
    me = lax.axis_index("dp")
    z = lax.axis_index("tensor")
    c = lax.rem(me, NC)
    y = lax.rem(me // NC, NY)
    x = me // (NC * NY)

    def dp_of(x_, y_, c_):
        return (x_ * NY + y_) * NC + c_

    def dev(d, z_):
        return {"dp": d, "tensor": z_}

    def at_x(o):
        return dev(dp_of(lax.rem(x + o, NX), y, c), z)

    def at_y(o):
        return dev(dp_of(x, lax.rem(y + o, NY), c), z)

    def at_z(o):
        return dev(me, lax.rem(z + o, NZ))

    def at_d(o):
        return dev(lax.rem(me + o + NDP, NDP), z)

    sibling = dev(dp_of(x, y, 1 - c), z)

    my_rows = pl.ds(pl.multiple_of(z * TOK_Z, TOK_Z), TOK_Z)
    small = []
    for i, (a, b) in enumerate(
        ((keeper_in, keeper), (target_in, target), (former_in, former), (live_in, live),
         (feat, feat_all.at[my_rows]))
    ):
        small.append(pltpu.make_async_copy(a, b, in_sem.at[i]))
        small[-1].start()
    local = []
    for k, (j0, nj, _) in enumerate(CHUNKS):
        cols = pl.ds(j0 * LANES, nj * LANES)
        local.append(pltpu.make_async_copy(og.at[:, cols], og_v.at[:, cols], og_sem.at[k]))
        local[-1].start()
    mine = []
    for a, st in enumerate((st0, st1, st2)):
        mine.append(pltpu.make_async_copy(st, states.at[FRONT + 5 * a + 2], st_loc.at[a]))
        mine[-1].start()

    barrier = pltpu.get_barrier_semaphore()
    peers = (
        [at_z(o) for o in range(1, NZ)]
        + [sibling]
        + [at_x(o) for o in range(1, NX)]
        + [at_y(o) for o in range(1, NY)]
        + [at_d(o) for o in OFFSETS]
    )
    for p in peers:
        pl.semaphore_signal(barrier, inc=1, device_id=p, device_id_type=pl.DeviceIdType.MESH)
    pl.semaphore_wait(barrier, len(peers))

    sent = []

    def send(src, dst, s_sem, r_sem, to):
        copy = pltpu.make_async_remote_copy(
            src_ref=src, dst_ref=dst, send_sem=s_sem, recv_sem=r_sem,
            device_id=to, device_id_type=pl.DeviceIdType.MESH,
        )
        copy.start()
        sent.append(copy)
        return copy

    gather = [
        send(feat, feat_all.at[my_rows], ag_s.at[o - 1], ag_r.at[o - 1], at_z(o))
        for o in (4, 3, 5, 2, 6, 1, 7)
    ]

    moved = []
    for a, st in enumerate((st0, st1, st2)):
        for i, o in enumerate(OFFSETS):
            moved.append(
                send(st, states.at[FRONT + 5 * a + 2 - o], st_s.at[4 * a + i], st_r.at[4 * a + i], at_d(o))
            )

    for copy in small:
        copy.wait()

    def add_up(ref, count, stop):
        return lax.fori_loop(
            0, count, lambda i, t: t + jnp.where(i < stop, ref[i], 0), jnp.int32(0)
        )

    low = jnp.minimum(me, NDP - 2)
    high = jnp.maximum(me - 1, 0)
    at_same = (me < NDP - 1) & (keeper[low] == me)
    at_before = (me > 0) & (keeper[high] == me)
    owner = at_same | at_before
    cursor = jnp.where(at_same, low, high)
    begin = jnp.where(
        at_same, add_up(target, NDP - 1, low), add_up(target, NDP - 1, high)
    )
    meta[0] = begin
    meta[1] = jnp.where(owner, jnp.where(at_same, target[low], target[high]), 0)
    meta[2] = begin - (me - 2) * BLOCK
    edge = add_up(former, NDP, me - 2)
    for i in range(5):
        s = me - 2 + i
        inside = (s >= 0) & (s < NDP)
        size = jnp.where(inside, former[jnp.clip(s, 0, NDP - 1)], 0)
        meta[3 + 2 * i] = edge
        meta[4 + 2 * i] = edge + size
        edge = edge + size
    live_count = jnp.where(owner, live[me], 0)

    for copy in gather:
        copy.wait_recv()

    tok = lax.broadcasted_iota(jnp.int32, (TOK, ROWS), 0)
    masked = jnp.where(tok < live_count, feat_all[...].astype(jnp.float32), 0.0).astype(jnp.bfloat16)
    out_row = lax.broadcasted_iota(jnp.int32, (ROWS, ROWS), 0)
    in_row = lax.broadcasted_iota(jnp.int32, (ROWS, ROWS), 1)
    for w, order in enumerate(("x", "y")):
        cc, b, i = out_row // 64, lax.rem(out_row // 2, 32), lax.rem(out_row, 2)
        if order == "x":
            bx, by = b // NY, lax.rem(b, NY)
        else:
            bx, by = lax.rem(b, NX), b // NX
        pick = (in_row == ((bx * NY + by) * NC + cc) * 2 + i).astype(jnp.float32).astype(jnp.bfloat16)
        mt[w] = lax.dot_general(
            pick, masked, (((1,), (1,)), ((), ())), preferred_element_type=jnp.float32
        ).astype(jnp.bfloat16)

    cores = []
    for k, (j0, nj, order) in enumerate(CHUNKS):
        local[k].wait()
        w = 0 if order == "x" else 1
        for j in range(0, nj, 2):
            out = jnp.dot(
                mt[w],
                og_v[:, (j0 + j) * LANES : (j0 + j + 2) * LANES],
                preferred_element_type=jnp.float32,
            )
            part[k][pl.ds(j, ROWS, stride=nj), :] = out[:, :LANES]
            part[k][pl.ds(j + 1, ROWS, stride=nj), :] = out[:, LANES:]
        half = 64 * nj
        cores.append(
            send(
                part[k].at[pl.ds(pl.multiple_of((1 - c) * half, half), half)],
                core[k], co_s.at[k], co_r.at[k], sibling,
            )
        )

    def plan(order):
        if order == "x":
            return NX, x, at_x, NY, y, at_y
        return NY, y, at_y, NX, x, at_x

    first = []
    for k, (j0, nj, order) in enumerate(CHUNKS):
        n1, i1, at1, n2, i2, at2 = plan(order)
        g1 = 64 * nj // n1
        half = 64 * nj
        cores[k].wait_recv()
        copies = []
        for o in list(range(1, n1)) + [0]:
            row = pl.multiple_of(lax.rem(i1 + o, n1) * g1, g1)
            core[k][pl.ds(row, g1)] = core[k][pl.ds(row, g1)] + part[k][pl.ds(pl.multiple_of(c * half + row, g1), g1)]
            if o:
                copies.append(
                    send(core[k].at[pl.ds(row, g1)], r1[k].at[pl.ds((o - 1) * g1, g1)],
                         s1_s.at[k, o - 1], s1_r.at[k, o - 1], at1(o))
                )
        first.append(copies)

    second = []
    for k, (j0, nj, order) in enumerate(CHUNKS):
        n1, i1, at1, n2, i2, at2 = plan(order)
        g1 = 64 * nj // n1
        g2 = 2 * nj
        for copy in first[k]:
            copy.wait_recv()
        copies = []
        for o in list(range(1, n2)) + [0]:
            row = pl.multiple_of(lax.rem(i2 + o, n2) * g2, g2)
            base = pl.multiple_of(i1 * g1 + row, g2)
            total = core[k][pl.ds(base, g2)]
            for q in range(n1 - 1):
                total = total + r1[k][pl.ds(pl.multiple_of(q * g1 + row, g2), g2)]
            spot = pl.ds(pl.multiple_of(c * 64 * nj + row, g2), g2)
            part[k][spot] = total
            if o:
                copies.append(
                    send(part[k].at[spot], r2[k].at[pl.ds((o - 1) * g2, g2)],
                         s2_s.at[k, o - 1], s2_r.at[k, o - 1], at2(o))
                )
        second.append(copies)

    third = []
    for k, (j0, nj, order) in enumerate(CHUNKS):
        n1, i1, at1, n2, i2, at2 = plan(order)
        g2 = 2 * nj
        for copy in second[k]:
            copy.wait_recv()
        total = part[k][pl.ds(pl.multiple_of(c * 64 * nj + i2 * g2, g2), g2)]
        for q in range(n2 - 1):
            total = total + r2[k][q * g2 : (q + 1) * g2]
        fin[k][2 * g2 : 3 * g2] = total
        third.append([
            send(fin[k].at[pl.ds(2 * g2, g2)], fin[k].at[pl.ds((2 - o) * g2, g2)],
                 rd_s.at[k, i], rd_r.at[k, i], at_d(o))
            for i, o in enumerate(OFFSETS)
        ])

    for k, (j0, nj, order) in enumerate(CHUNKS):
        for copy in third[k]:
            copy.wait_recv()
        for m in range(10):
            grad[m * COLS + j0 : m * COLS + j0 + nj] = fin[k][m * nj : (m + 1) * nj]

    for copy in moved:
        copy.wait_recv()
    for copy in sent:
        copy.wait_send()
    for copy in mine:
        copy.wait()


def gather_and_reduce(features, og, live, former, target, keeper, st0, st1, st2):
    n = len(CHUNKS)
    vmem = lambda rows, dtype=jnp.float32: pltpu.VMEM((rows, LANES), dtype)
    scratch = [
        pltpu.VMEM((TOK, COLS * LANES), jnp.bfloat16),
        vmem(TOK, jnp.bfloat16),
        pltpu.VMEM((2, ROWS, TOK), jnp.bfloat16),
    ] + [pltpu.SMEM(v.shape, jnp.int32) for v in (live, keeper, former, target)]
    counts = [(NX, NY) if order == "x" else (NY, NX) for _, _, order in CHUNKS]
    scratch += [vmem(ROWS * nj) for _, nj, _ in CHUNKS]
    scratch += [vmem(64 * nj) for _, nj, _ in CHUNKS]
    scratch += [vmem((n1 - 1) * 64 * nj // n1) for (_, nj, _), (n1, n2) in zip(CHUNKS, counts)]
    scratch += [vmem((n2 - 1) * 2 * nj) for (_, nj, _), (n1, n2) in zip(CHUNKS, counts)]
    scratch += [vmem(10 * nj) for _, nj, _ in CHUNKS]
    dma = lambda *s: pltpu.SemaphoreType.DMA(s)
    scratch += [
        dma(7), dma(7), dma(n), dma(12), dma(12), dma(3), dma(n), dma(n),
        dma(n, 7), dma(n, 7), dma(n, 7), dma(n, 7), dma(n, 4), dma(n, 4), dma(5),
    ]
    smem = pl.BlockSpec(memory_space=pltpu.SMEM)
    anyw = pl.BlockSpec(memory_space=pl.ANY)
    return pl.pallas_call(
        main_kernel,
        out_shape=(
            jax.ShapeDtypeStruct((SLOTS, 1, OLD_CAP), jnp.float32),
            jax.ShapeDtypeStruct((GRAD_ROWS, LANES), jnp.float32),
            jax.ShapeDtypeStruct((16,), jnp.int32),
        ),
        in_specs=[pl.BlockSpec(memory_space=pltpu.HBM)] * 9,
        out_specs=(anyw, pl.BlockSpec(memory_space=pltpu.VMEM), smem),
        scratch_shapes=scratch,
        compiler_params=pltpu.CompilerParams(
            collective_id=0, has_side_effects=True, vmem_limit_bytes=40 * 1024 * 1024
        ),
        cost_estimate=pl.CostEstimate(flops=2 * TOK * ROWS * COLS * LANES, bytes_accessed=6_000_000, transcendentals=0),
    )(live, keeper, former, target, features, og, st0, st1, st2)


def update_kernel(meta, states, grad, out_master, out_first, out_second):
    lane = lax.broadcasted_iota(jnp.int32, (WIN, LANES), 1)
    slot = lax.broadcasted_iota(jnp.int32, (WIN, LANES), 0) * LANES + lane
    begin, length = meta[0], meta[1]
    live = slot < length
    place = slot + begin

    def window(ref, row, shift):
        back = lax.rem(LANES - shift, LANES)
        here = pltpu.roll(ref[pl.ds(row, WIN), :], back, 1)
        after = pltpu.roll(ref[pl.ds(row + 1, WIN), :], back, 1)
        return jnp.where(lane < LANES - shift, here, after)

    delta = meta[2]
    row = jnp.clip(delta >> 7, 0, GRAD_ROWS - WIN - 1)
    gradient = jnp.where(live, window(grad, row, delta & 127), 0.0)

    gathered = [jnp.zeros((WIN, LANES), jnp.float32)] * 3
    for i in range(5):
        lower, upper = meta[3 + 2 * i], meta[4 + 2 * i]
        inside = (place >= lower) & (place < upper) & live
        delta = begin - lower
        row = jnp.clip(delta >> 7, -OUT_ROWS, OLD_ROWS)
        for a in range(3):
            base = (FRONT + 5 * a + i) * OLD_ROWS
            gathered[a] = jnp.where(inside, window(states, base + row, delta & 127), gathered[a])

    master, one, two = gathered
    first_next = BETA_ONE * one + (1.0 - BETA_ONE) * gradient
    second_next = BETA_TWO * two + (1.0 - BETA_TWO) * gradient * gradient
    update = first_next / CORRECT_ONE / (jnp.sqrt(second_next / CORRECT_TWO) + EPSILON)
    master_next = master - LEARN_RATE * (update + DECAY * master)
    for value, out in ((master_next, out_master), (first_next, out_first), (second_next, out_second)):
        value = jnp.where(live, value, 0.0)
        for t in range(OUT_ROWS):
            wide = min(LANES, NEW_CAP - t * LANES)
            out[:, t * LANES : t * LANES + wide] = value[t : t + 1, :wide]


def on_device(features, og, live, former, target, keeper, st0, st1, st2):
    states, grad, meta = gather_and_reduce(features, og, live, former, target, keeper, st0, st1, st2)
    states = states.reshape(SLOTS * OLD_ROWS, LANES)
    vm = pl.BlockSpec(memory_space=pltpu.VMEM)
    return pl.pallas_call(
        update_kernel,
        out_shape=[jax.ShapeDtypeStruct((1, NEW_CAP), jnp.float32)] * 3,
        in_specs=[pl.BlockSpec(memory_space=pltpu.SMEM), vm, vm],
        out_specs=[vm] * 3,
        compiler_params=pltpu.CompilerParams(vmem_limit_bytes=16 * 1024 * 1024),
        cost_estimate=pl.CostEstimate(flops=1_000_000, bytes_accessed=1_400_000, transcendentals=0),
    )(meta, states, grad)


def solution(mesh):
    placed = (
        P(("dp", "tensor"), None),
        P("dp", "tensor"),
        P(),
        P(),
        P(),
        P(),
        P("tensor", "dp"),
        P("tensor", "dp"),
        P("tensor", "dp"),
    )
    return jax.shard_map(
        on_device,
        mesh=mesh,
        in_specs=placed,
        out_specs=(P("tensor", "dp"), P("tensor", "dp"), P("tensor", "dp")),
        check_vma=False,
    )
```

time: 276 us -> 54.6 us (0.20)
  waiting for transfers between devices: 184 us -> 0 us
  Pallas kernels: 0 us -> 45.8 us
  between operations: 32.1 us -> 0.66 us
  blocking collectives: 25.9 us -> 0 us
  other arithmetic: 13.4 us -> 0 us
  starting transfers between devices: 8.56 us -> 0 us
  matrix products: 2.81 us -> 0 us
    unnamed x2 -> x0, waiting for transfers between devices: 177 us -> none
    pallas_call x0 -> x2, Pallas kernels: none -> 45.8 us  [the longest x1 44 us: gather_and_reduce(): pl.pallas_call(main_kernel, out_shape=(jax.ShapeDtypeStruct((SLOTS, 1, OL...]
    all_gather x1 -> x0, blocking collectives: 25.9 us -> none  [on_device(): features_all = lax.all_gather(features, 'tensor', axis=0, tiled=True)]
    ppermute x4 -> x0, starting transfers between devices: 8.52 us -> none  [passed_along(): lax.ppermute(value, axis, [(source, source + steps) for source in range(i...]
    ppermute x4 -> x0, waiting for transfers between devices: 7.34 us -> none  [passed_along(): lax.ppermute(value, axis, [(source, source + steps) for source in range(i...]
    and x4 -> x0, other arithmetic: 6.23 us -> none  [the longest x3 4.94 us: read_range(): (positions >= anchor) & (positions < upper_edge) & (slot_ids < length)]
    unnamed x14 -> x18, local copies, waits for them, and re-layouts: 2.06 us -> 7.77 us
    select_n x2 -> x0, other arithmetic: 3.29 us -> none  [the longest x1 2.32 us: adamw_step(): jnp.where(in_range, second_next, jnp.zeros_like(second_next))]
  transfers between devices with their start and end apart: 5 -> 0, of which waited for: 3 -> 0; matrix products, arithmetic and copies ran while one was open for 3% -> 0% of each run, Pallas kernels for 0% -> 0%
where the time goes in v1:
time: 54.6 us; the launch traced here: 54.2 us
  Pallas kernels  45.8 us (84%)
  local copies, waits for them, and re-layouts  7.77 us (14%)
  between operations  0.66 us (1%)
    pallas_call x1, Pallas kernels, gather_and_reduce(): pl.pallas_call(main_kernel, out_shape=(jax.ShapeDtypeStruct((SLOTS, 1, OL...  44 us
    unnamed x18, local copies, waits for them, and re-layouts  7.77 us
    pallas_call x1, Pallas kernels, on_device(): pl.pallas_call(update_kernel, out_shape=[jax.ShapeDtypeStruct((1, NEW_CAP...  1.83 us

profile of v1, /device:TPU:1, one launch (start us, length us, event | category | flops | bytes accessed | tf_op | source)
XLA Modules:
  0.0 54.2 jit_solution(1151946335316006731)
XLA Ops:
  0.6 0.0 copy-start
  0.6 2.0 %copy-done = bf16[512,3584]{1,0:T(8,128)(2,1)S(1)} copy-done((bf16[512,3584]{1,0:T(8,128)(2,1)S(1)}, bf16[512,3584]{1,0:T(8,128)(2,1)}, u32[]{:S(2)}) %copy-start) | copy-done | bytes 3670040
  2.7 0.0 copy-start.1
  2.7 0.8 %copy-done.1 = f32[1,12544]{1,0:T(1,128)S(1)} copy-done((f32[1,12544]{1,0:T(1,128)S(1)}, f32[1,12544]{1,0:T(1,128)}, u32[]{:S(2)}) %copy-start.1) | copy-done | bytes 50200
  3.5 0.0 copy-start.2
  3.5 0.8 %copy-done.2 = f32[1,12544]{1,0:T(1,128)S(1)} copy-done((f32[1,12544]{1,0:T(1,128)S(1)}, f32[1,12544]{1,0:T(1,128)}, u32[]{:S(2)}) %copy-start.2) | copy-done | bytes 50200
  4.3 0.0 copy-start.3
  4.3 0.8 %copy-done.3 = f32[1,12544]{1,0:T(1,128)S(1)} copy-done((f32[1,12544]{1,0:T(1,128)S(1)}, f32[1,12544]{1,0:T(1,128)}, u32[]{:S(2)}) %copy-start.3) | copy-done | bytes 50200
  5.1 0.0 copy-start.4
  5.1 0.7 %copy-done.4 = bf16[64,128]{1,0:T(8,128)(2,1)S(1)} copy-done((bf16[64,128]{1,0:T(8,128)(2,1)S(1)}, bf16[64,128]{1,0:T(8,128)(2,1)}, u32[]{:S(2)}) %copy-start.4) | copy-done | bytes 16408
  5.8 0.0 copy-start.5
  5.8 0.7 %copy-done.5 = s32[64]{0:T(128)S(1)} copy-done((s32[64]{0:T(128)S(1)}, s32[64]{0:T(128)}, u32[]{:S(2)}) %copy-start.5) | copy-done | bytes 280
  6.5 0.0 copy-start.6
  6.5 0.7 %copy-done.6 = s32[63]{0:T(128)S(1)} copy-done((s32[63]{0:T(128)S(1)}, s32[63]{0:T(128)}, u32[]{:S(2)}) %copy-start.6) | copy-done | bytes 276
  7.1 0.0 copy-start.7
  7.1 0.7 %copy-done.7 = s32[64]{0:T(128)S(1)} copy-done((s32[64]{0:T(128)S(1)}, s32[64]{0:T(128)}, u32[]{:S(2)}) %copy-start.7) | copy-done | bytes 280
  7.8 0.0 copy-start.8
  7.8 0.7 %copy-done.8 = s32[63]{0:T(128)S(1)} copy-done((s32[63]{0:T(128)S(1)}, s32[63]{0:T(128)}, u32[]{:S(2)}) %copy-start.8) | copy-done | bytes 276
  8.4 44.0 %shard_map.112 = (f32[20,1,12544]{2,1,0:T(1,128)S(1)}, f32[304,128]{1,0:T(8,128)S(1)}, s32[16]{0:T(128)S(1)}) custom-call(s32[64]{0:T(128)S(1)} %copy-done.5, s32[63]{0:T(128)S(1)} %copy-done.6, s32[64]{0:T(128)S(1)} %copy-done.7, s32[63]{0:T(128)S(1)} %copy-done.8, bf16[64,128]{1,0:T(8,128)(2,1)S(1)} %copy-done.4, bf16[512,3584]{1,0:T(8,128)(2,1)S(1)} %copy-done, ...), custom_call_target="tpu_custom_call" | custom-call | flops 469762048 | bytes 6000000 | tf_op jit(solution)/shard_map/pallas_call | solution.py:290
  52.4 1.8 %shard_map.113 = (f32[1,12659]{1,0:T(1,128)}, f32[1,12659]{1,0:T(1,128)}, f32[1,12659]{1,0:T(1,128)}) custom-call(s32[16]{0:T(128)S(1)} %get-tuple-element.6.meta, f32[1960,128]{1,0:T(8,128)S(1)} %bitcast.1, f32[304,128]{1,0:T(8,128)S(1)} %get-tuple-element.8.grad), custom_call_target="tpu_custom_call" | custom-call | flops 1000000 | bytes 1400000 | tf_op jit(solution)/shard_map/pallas_call | solution.py:350
Async XLA Ops:
  0.6 2.0 %copy-start = (bf16[512,3584]{1,0:T(8,128)(2,1)S(1)}, bf16[512,3584]{1,0:T(8,128)(2,1)}, u32[]{:S(2)}) copy-start(bf16[512,3584]{1,0:T(8,128)(2,1)} %og.1) | copy-start | bytes 11010052
  2.7 0.8 %copy-start.1 = (f32[1,12544]{1,0:T(1,128)S(1)}, f32[1,12544]{1,0:T(1,128)}, u32[]{:S(2)}) copy-start(f32[1,12544]{1,0:T(1,128)} %st0.1) | copy-start | bytes 150532
  3.5 0.8 %copy-start.2 = (f32[1,12544]{1,0:T(1,128)S(1)}, f32[1,12544]{1,0:T(1,128)}, u32[]{:S(2)}) copy-start(f32[1,12544]{1,0:T(1,128)} %st1.1) | copy-start | bytes 150532
  4.3 0.8 %copy-start.3 = (f32[1,12544]{1,0:T(1,128)S(1)}, f32[1,12544]{1,0:T(1,128)}, u32[]{:S(2)}) copy-start(f32[1,12544]{1,0:T(1,128)} %st2.1) | copy-start | bytes 150532
  5.1 0.7 %copy-start.4 = (bf16[64,128]{1,0:T(8,128)(2,1)S(1)}, bf16[64,128]{1,0:T(8,128)(2,1)}, u32[]{:S(2)}) copy-start(bf16[64,128]{1,0:T(8,128)(2,1)} %feat.1) | copy-start | bytes 49156
  5.8 0.7 %copy-start.5 = (s32[64]{0:T(128)S(1)}, s32[64]{0:T(128)}, u32[]{:S(2)}) copy-start(s32[64]{0:T(128)} %live_in.1) | copy-start | bytes 772
  6.5 0.7 %copy-start.6 = (s32[63]{0:T(128)S(1)}, s32[63]{0:T(128)}, u32[]{:S(2)}) copy-start(s32[63]{0:T(128)} %keeper_in.1) | copy-start | bytes 760
  7.1 0.7 %copy-start.7 = (s32[64]{0:T(128)S(1)}, s32[64]{0:T(128)}, u32[]{:S(2)}) copy-start(s32[64]{0:T(128)} %former_in.1) | copy-start | bytes 772
  7.8 0.7 %copy-start.8 = (s32[63]{0:T(128)S(1)}, s32[63]{0:T(128)}, u32[]{:S(2)}) copy-start(s32[63]{0:T(128)} %target_in.1) | copy-start | bytes 760

commit v2 on v1

--- a/solution.py
+++ b/solution.py
@@ -33,12 +33,25 @@
 FRONT = 2
 OFFSETS = (-2, -1, 1, 2)
 
-CHUNKS = ((0, 20, "x"), (20, 8, "y"))
+CHUNKS = ((0, 12, "x"), (12, 8, "x"), (20, 8, "y"))
+
+
+def slot_ids():
+    row = lax.broadcasted_iota(jnp.int32, (WIN, LANES), 0)
+    return row * LANES + lax.broadcasted_iota(jnp.int32, (WIN, LANES), 1)
+
+
+def window(ref, row, shift):
+    lane = lax.broadcasted_iota(jnp.int32, (WIN, LANES), 1)
+    back = lax.rem(LANES - shift, LANES)
+    here = pltpu.roll(ref[pl.ds(row, WIN), :], back, 1)
+    after = pltpu.roll(ref[pl.ds(row + 1, WIN), :], back, 1)
+    return jnp.where(lane < LANES - shift, here, after)
 
 
 def main_kernel(
-    live_in, keeper_in, former_in, target_in, feat, og, st0, st1, st2, states, grad, meta,
-    og_v, feat_all, mt, live, keeper, former, target, *rest,
+    live_in, keeper_in, former_in, target_in, feat, og, st0, st1, st2, slots, grad, meta,
+    states, old, og_v, feat_all, mt, live, keeper, former, target, *rest,
 ):
     n = len(CHUNKS)
     part, core, r1, r2, fin = (rest[k * n : (k + 1) * n] for k in range(5))
@@ -85,7 +98,7 @@
         local[-1].start()
     mine = []
     for a, st in enumerate((st0, st1, st2)):
-        mine.append(pltpu.make_async_copy(st, states.at[FRONT + 5 * a + 2], st_loc.at[a]))
+        mine.append(pltpu.make_async_copy(st, states.at[5 * a + 2], st_loc.at[a]))
         mine[-1].start()
 
     barrier = pltpu.get_barrier_semaphore()
@@ -120,7 +133,7 @@
     for a, st in enumerate((st0, st1, st2)):
         for i, o in enumerate(OFFSETS):
             moved.append(
-                send(st, states.at[FRONT + 5 * a + 2 - o], st_s.at[4 * a + i], st_r.at[4 * a + i], at_d(o))
+                send(st, states.at[5 * a + 2 - o], st_s.at[4 * a + i], st_r.at[4 * a + i], at_d(o))
             )
 
     for copy in small:
@@ -140,16 +153,16 @@
     begin = jnp.where(
         at_same, add_up(target, NDP - 1, low), add_up(target, NDP - 1, high)
     )
-    meta[0] = begin
-    meta[1] = jnp.where(owner, jnp.where(at_same, target[low], target[high]), 0)
-    meta[2] = begin - (me - 2) * BLOCK
+    length = jnp.where(owner, jnp.where(at_same, target[low], target[high]), 0)
+    meta[0] = length
+    meta[1] = begin - (me - 2) * BLOCK
+    edges = []
     edge = add_up(former, NDP, me - 2)
     for i in range(5):
         s = me - 2 + i
         inside = (s >= 0) & (s < NDP)
         size = jnp.where(inside, former[jnp.clip(s, 0, NDP - 1)], 0)
-        meta[3 + 2 * i] = edge
-        meta[4 + 2 * i] = edge + size
+        edges.append((edge, edge + size))
         edge = edge + size
     live_count = jnp.where(owner, live[me], 0)
 
@@ -212,6 +225,26 @@
                          s1_s.at[k, o - 1], s1_r.at[k, o - 1], at1(o))
                 )
         first.append(copies)
+
+    for copy in mine:
+        copy.wait()
+    for copy in moved:
+        copy.wait_recv()
+    for i in range(15):
+        first_row = (FRONT + i) * OLD_ROWS
+        old[first_row : first_row + OLD_ROWS] = states[i].reshape(OLD_ROWS, LANES)
+    slot = slot_ids()
+    place = slot + begin
+    gathered = [jnp.zeros((WIN, LANES), jnp.float32)] * 3
+    for i, (lower, upper) in enumerate(edges):
+        inside = (place >= lower) & (place < upper) & (slot < length)
+        delta = begin - lower
+        row = jnp.clip(delta >> 7, -OUT_ROWS, OLD_ROWS)
+        for a in range(3):
+            base = (FRONT + 5 * a + i) * OLD_ROWS
+            gathered[a] = jnp.where(inside, window(old, base + row, delta & 127), gathered[a])
+    for a in range(3):
+        slots[a * WIN : (a + 1) * WIN] = gathered[a]
 
     second = []
     for k, (j0, nj, order) in enumerate(CHUNKS):
@@ -258,18 +291,16 @@
         for m in range(10):
             grad[m * COLS + j0 : m * COLS + j0 + nj] = fin[k][m * nj : (m + 1) * nj]
 
-    for copy in moved:
-        copy.wait_recv()
     for copy in sent:
         copy.wait_send()
-    for copy in mine:
-        copy.wait()
 
 
 def gather_and_reduce(features, og, live, former, target, keeper, st0, st1, st2):
     n = len(CHUNKS)
     vmem = lambda rows, dtype=jnp.float32: pltpu.VMEM((rows, LANES), dtype)
     scratch = [
+        pltpu.VMEM((15, 1, OLD_CAP), jnp.float32),
+        vmem(SLOTS * OLD_ROWS),
         pltpu.VMEM((TOK, COLS * LANES), jnp.bfloat16),
         vmem(TOK, jnp.bfloat16),
         pltpu.VMEM((2, ROWS, TOK), jnp.bfloat16),
@@ -286,52 +317,40 @@
         dma(n, 7), dma(n, 7), dma(n, 7), dma(n, 7), dma(n, 4), dma(n, 4), dma(5),
     ]
     smem = pl.BlockSpec(memory_space=pltpu.SMEM)
-    anyw = pl.BlockSpec(memory_space=pl.ANY)
+    vm = pl.BlockSpec(memory_space=pltpu.VMEM)
     return pl.pallas_call(
         main_kernel,
         out_shape=(
-            jax.ShapeDtypeStruct((SLOTS, 1, OLD_CAP), jnp.float32),
+            jax.ShapeDtypeStruct((3 * WIN, LANES), jnp.float32),
             jax.ShapeDtypeStruct((GRAD_ROWS, LANES), jnp.float32),
-            jax.ShapeDtypeStruct((16,), jnp.int32),
+            jax.ShapeDtypeStruct((2,), jnp.int32),
         ),
         in_specs=[pl.BlockSpec(memory_space=pltpu.HBM)] * 9,
-        out_specs=(anyw, pl.BlockSpec(memory_space=pltpu.VMEM), smem),
+        out_specs=(vm, vm, smem),
         scratch_shapes=scratch,
         compiler_params=pltpu.CompilerParams(
-            collective_id=0, has_side_effects=True, vmem_limit_bytes=40 * 1024 * 1024
+            collective_id=0, has_side_effects=True, vmem_limit_bytes=56 * 1024 * 1024
         ),
         cost_estimate=pl.CostEstimate(flops=2 * TOK * ROWS * COLS * LANES, bytes_accessed=6_000_000, transcendentals=0),
     )(live, keeper, former, target, features, og, st0, st1, st2)
 
 
-def update_kernel(meta, states, grad, out_master, out_first, out_second):
-    lane = lax.broadcasted_iota(jnp.int32, (WIN, LANES), 1)
-    slot = lax.broadcasted_iota(jnp.int32, (WIN, LANES), 0) * LANES + lane
-    begin, length = meta[0], meta[1]
-    live = slot < length
-    place = slot + begin
-
-    def window(ref, row, shift):
-        back = lax.rem(LANES - shift, LANES)
-        here = pltpu.roll(ref[pl.ds(row, WIN), :], back, 1)
-        after = pltpu.roll(ref[pl.ds(row + 1, WIN), :], back, 1)
-        return jnp.where(lane < LANES - shift, here, after)
-
-    delta = meta[2]
+def update_kernel(
+    meta_in, slots_in, grad_in, out_master, out_first, out_second, meta, slots, grad, sem
+):
+    copies = [
+        pltpu.make_async_copy(a, b, sem.at[i])
+        for i, (a, b) in enumerate(((meta_in, meta), (slots_in, slots), (grad_in, grad)))
+    ]
+    for copy in copies:
+        copy.start()
+    for copy in copies:
+        copy.wait()
+    live = slot_ids() < meta[0]
+    delta = meta[1]
     row = jnp.clip(delta >> 7, 0, GRAD_ROWS - WIN - 1)
     gradient = jnp.where(live, window(grad, row, delta & 127), 0.0)
-
-    gathered = [jnp.zeros((WIN, LANES), jnp.float32)] * 3
-    for i in range(5):
-        lower, upper = meta[3 + 2 * i], meta[4 + 2 * i]
-        inside = (place >= lower) & (place < upper) & live
-        delta = begin - lower
-        row = jnp.clip(delta >> 7, -OUT_ROWS, OLD_ROWS)
-        for a in range(3):
-            base = (FRONT + 5 * a + i) * OLD_ROWS
-            gathered[a] = jnp.where(inside, window(states, base + row, delta & 127), gathered[a])
-
-    master, one, two = gathered
+    master, one, two = (slots[a * WIN : (a + 1) * WIN] for a in range(3))
     first_next = BETA_ONE * one + (1.0 - BETA_ONE) * gradient
     second_next = BETA_TWO * two + (1.0 - BETA_TWO) * gradient * gradient
     update = first_next / CORRECT_ONE / (jnp.sqrt(second_next / CORRECT_TWO) + EPSILON)
@@ -344,17 +363,22 @@
 
 
 def on_device(features, og, live, former, target, keeper, st0, st1, st2):
-    states, grad, meta = gather_and_reduce(features, og, live, former, target, keeper, st0, st1, st2)
-    states = states.reshape(SLOTS * OLD_ROWS, LANES)
+    slots, grad, meta = gather_and_reduce(features, og, live, former, target, keeper, st0, st1, st2)
     vm = pl.BlockSpec(memory_space=pltpu.VMEM)
     return pl.pallas_call(
         update_kernel,
         out_shape=[jax.ShapeDtypeStruct((1, NEW_CAP), jnp.float32)] * 3,
-        in_specs=[pl.BlockSpec(memory_space=pltpu.SMEM), vm, vm],
+        in_specs=[pl.BlockSpec(memory_space=pl.ANY)] * 3,
         out_specs=[vm] * 3,
-        compiler_params=pltpu.CompilerParams(vmem_limit_bytes=16 * 1024 * 1024),
+        scratch_shapes=[
+            pltpu.SMEM(meta.shape, meta.dtype),
+            pltpu.VMEM(slots.shape, slots.dtype),
+            pltpu.VMEM(grad.shape, grad.dtype),
+            pltpu.SemaphoreType.DMA((3,)),
+        ],
+        compiler_params=pltpu.CompilerParams(vmem_limit_bytes=56 * 1024 * 1024),
         cost_estimate=pl.CostEstimate(flops=1_000_000, bytes_accessed=1_400_000, transcendentals=0),
-    )(meta, states, grad)
+    )(meta, slots, grad)
 
 
 def solution(mesh):

time: 54.6 us -> 44.9 us (0.82)
  local copies, waits for them, and re-layouts: 7.77 us -> 0 us
  Pallas kernels: 45.8 us -> 44.2 us
    unnamed x18 -> x0, local copies, waits for them, and re-layouts: 7.77 us -> none
    pallas_call x1, Pallas kernels: 44 us -> 42.3 us  [gather_and_reduce(): pl.pallas_call(main_kernel, out_shape=(jax.ShapeDtypeStruct((3 * WIN, LAN...]
where the time goes in v2:
time: 44.9 us; the launch traced here: 44.8 us
  Pallas kernels  44.2 us (98%)
  between operations  0.64 us (1%)
    pallas_call x1, Pallas kernels, gather_and_reduce(): pl.pallas_call(main_kernel, out_shape=(jax.ShapeDtypeStruct((3 * WIN, LAN...  42.3 us
    pallas_call x1, Pallas kernels, on_device(): pl.pallas_call(update_kernel, out_shape=[jax.ShapeDtypeStruct((1, NEW_CAP...  1.87 us

profile of v2, /device:TPU:1, one launch (start us, length us, event | category | flops | bytes accessed | tf_op | source)
XLA Modules:
  0.0 44.8 jit_solution(5768069072687395320)
XLA Ops:
  0.6 42.3 %shard_map.112 = (f32[312,128]{1,0:T(8,128)}, f32[304,128]{1,0:T(8,128)}, s32[2]{0:T(128)}) custom-call(s32[64]{0:T(128)} %live_in.1, s32[63]{0:T(128)} %keeper_in.1, s32[64]{0:T(128)} %former_in.1, s32[63]{0:T(128)} %target_in.1, bf16[64,128]{1,0:T(8,128)(2,1)} %feat.1, bf16[512,3584]{1,0:T(8,128)(2,1)} %og.1, f32[1,12544]{1,0:T(1,128)} %st0.1, ...), custom_call_target="tpu_custom_call" | custom-call | flops 469762048 | bytes 6000000 | tf_op jit(solution)/shard_map/pallas_call | solution.py:321
  42.9 1.9 %shard_map.113 = (f32[1,12659]{1,0:T(1,128)}, f32[1,12659]{1,0:T(1,128)}, f32[1,12659]{1,0:T(1,128)}) custom-call(s32[2]{0:T(128)} %get-tuple-element.6.meta_in, f32[312,128]{1,0:T(8,128)} %get-tuple-element.7.slots_in, f32[304,128]{1,0:T(8,128)} %get-tuple-element.8.grad_in), custom_call_target="tpu_custom_call" | custom-call | flops 1000000 | bytes 1400000 | tf_op jit(solution)/shard_map/pallas_call | solution.py:368

commit v3 on v2

--- a/solution.py
+++ b/solution.py
@@ -50,8 +50,8 @@
 
 
 def main_kernel(
-    live_in, keeper_in, former_in, target_in, feat, og, st0, st1, st2, slots, grad, meta,
-    states, old, og_v, feat_all, mt, live, keeper, former, target, *rest,
+    live_in, keeper_in, former_in, target_in, feat, og, st0, st1, st2, slots,
+    states, old, kept, grad, pick, og_v, feat_all, mt, live, keeper, former, target, *rest,
 ):
     n = len(CHUNKS)
     part, core, r1, r2, fin = (rest[k * n : (k + 1) * n] for k in range(5))
@@ -83,6 +83,16 @@
 
     sibling = dev(dp_of(x, y, 1 - c), z)
 
+    barrier = pltpu.get_barrier_semaphore()
+    peers = (
+        [at_z(o) for o in range(1, NZ)]
+        + [sibling]
+        + [at_x(o) for o in range(1, NX)]
+        + [at_y(o) for o in range(1, NY)]
+        + [at_d(o) for o in OFFSETS]
+    )
+    for p in peers:
+        pl.semaphore_signal(barrier, inc=1, device_id=p, device_id_type=pl.DeviceIdType.MESH)
     my_rows = pl.ds(pl.multiple_of(z * TOK_Z, TOK_Z), TOK_Z)
     small = []
     for i, (a, b) in enumerate(
@@ -101,16 +111,6 @@
         mine.append(pltpu.make_async_copy(st, states.at[5 * a + 2], st_loc.at[a]))
         mine[-1].start()
 
-    barrier = pltpu.get_barrier_semaphore()
-    peers = (
-        [at_z(o) for o in range(1, NZ)]
-        + [sibling]
-        + [at_x(o) for o in range(1, NX)]
-        + [at_y(o) for o in range(1, NY)]
-        + [at_d(o) for o in OFFSETS]
-    )
-    for p in peers:
-        pl.semaphore_signal(barrier, inc=1, device_id=p, device_id_type=pl.DeviceIdType.MESH)
     pl.semaphore_wait(barrier, len(peers))
 
     sent = []
@@ -154,8 +154,6 @@
         at_same, add_up(target, NDP - 1, low), add_up(target, NDP - 1, high)
     )
     length = jnp.where(owner, jnp.where(at_same, target[low], target[high]), 0)
-    meta[0] = length
-    meta[1] = begin - (me - 2) * BLOCK
     edges = []
     edge = add_up(former, NDP, me - 2)
     for i in range(5):
@@ -166,11 +164,6 @@
         edge = edge + size
     live_count = jnp.where(owner, live[me], 0)
 
-    for copy in gather:
-        copy.wait_recv()
-
-    tok = lax.broadcasted_iota(jnp.int32, (TOK, ROWS), 0)
-    masked = jnp.where(tok < live_count, feat_all[...].astype(jnp.float32), 0.0).astype(jnp.bfloat16)
     out_row = lax.broadcasted_iota(jnp.int32, (ROWS, ROWS), 0)
     in_row = lax.broadcasted_iota(jnp.int32, (ROWS, ROWS), 1)
     for w, order in enumerate(("x", "y")):
@@ -179,9 +172,16 @@
             bx, by = b // NY, lax.rem(b, NY)
         else:
             bx, by = lax.rem(b, NX), b // NX
-        pick = (in_row == ((bx * NY + by) * NC + cc) * 2 + i).astype(jnp.float32).astype(jnp.bfloat16)
+        pick[w] = (in_row == ((bx * NY + by) * NC + cc) * 2 + i).astype(jnp.float32).astype(jnp.bfloat16)
+
+    for copy in gather:
+        copy.wait_recv()
+
+    tok = lax.broadcasted_iota(jnp.int32, (TOK, ROWS), 0)
+    masked = jnp.where(tok < live_count, feat_all[...].astype(jnp.float32), 0.0).astype(jnp.bfloat16)
+    for w in range(2):
         mt[w] = lax.dot_general(
-            pick, masked, (((1,), (1,)), ((), ())), preferred_element_type=jnp.float32
+            pick[w], masked, (((1,), (1,)), ((), ())), preferred_element_type=jnp.float32
         ).astype(jnp.bfloat16)
 
     cores = []
@@ -244,7 +244,7 @@
             base = (FRONT + 5 * a + i) * OLD_ROWS
             gathered[a] = jnp.where(inside, window(old, base + row, delta & 127), gathered[a])
     for a in range(3):
-        slots[a * WIN : (a + 1) * WIN] = gathered[a]
+        kept[a] = gathered[a]
 
     second = []
     for k, (j0, nj, order) in enumerate(CHUNKS):
@@ -291,6 +291,18 @@
         for m in range(10):
             grad[m * COLS + j0 : m * COLS + j0 + nj] = fin[k][m * nj : (m + 1) * nj]
 
+    live_slot = slot_ids() < length
+    delta = begin - (me - 2) * BLOCK
+    row = jnp.clip(delta >> 7, 0, GRAD_ROWS - WIN - 1)
+    gradient = jnp.where(live_slot, window(grad, row, delta & 127), 0.0)
+    master, one, two = kept[0], kept[1], kept[2]
+    first_next = BETA_ONE * one + (1.0 - BETA_ONE) * gradient
+    second_next = BETA_TWO * two + (1.0 - BETA_TWO) * gradient * gradient
+    update = first_next / CORRECT_ONE / (jnp.sqrt(second_next / CORRECT_TWO) + EPSILON)
+    master_next = master - LEARN_RATE * (update + DECAY * master)
+    for a, value in enumerate((master_next, first_next, second_next)):
+        slots[a * WIN : (a + 1) * WIN] = jnp.where(live_slot, value, 0.0)
+
     for copy in sent:
         copy.wait_send()
 
@@ -301,6 +313,9 @@
     scratch = [
         pltpu.VMEM((15, 1, OLD_CAP), jnp.float32),
         vmem(SLOTS * OLD_ROWS),
+        pltpu.VMEM((3, WIN, LANES), jnp.float32),
+        vmem(GRAD_ROWS),
+        pltpu.VMEM((2, ROWS, ROWS), jnp.bfloat16),
         pltpu.VMEM((TOK, COLS * LANES), jnp.bfloat16),
         vmem(TOK, jnp.bfloat16),
         pltpu.VMEM((2, ROWS, TOK), jnp.bfloat16),
@@ -316,17 +331,12 @@
         dma(7), dma(7), dma(n), dma(12), dma(12), dma(3), dma(n), dma(n),
         dma(n, 7), dma(n, 7), dma(n, 7), dma(n, 7), dma(n, 4), dma(n, 4), dma(5),
     ]
-    smem = pl.BlockSpec(memory_space=pltpu.SMEM)
     vm = pl.BlockSpec(memory_space=pltpu.VMEM)
     return pl.pallas_call(
         main_kernel,
-        out_shape=(
-            jax.ShapeDtypeStruct((3 * WIN, LANES), jnp.float32),
-            jax.ShapeDtypeStruct((GRAD_ROWS, LANES), jnp.float32),
-            jax.ShapeDtypeStruct((2,), jnp.int32),
-        ),
+        out_shape=jax.ShapeDtypeStruct((3 * WIN, LANES), jnp.float32),
         in_specs=[pl.BlockSpec(memory_space=pltpu.HBM)] * 9,
-        out_specs=(vm, vm, smem),
+        out_specs=vm,
         scratch_shapes=scratch,
         compiler_params=pltpu.CompilerParams(
             collective_id=0, has_side_effects=True, vmem_limit_bytes=56 * 1024 * 1024
@@ -335,50 +345,35 @@
     )(live, keeper, former, target, features, og, st0, st1, st2)
 
 
-def update_kernel(
-    meta_in, slots_in, grad_in, out_master, out_first, out_second, meta, slots, grad, sem
-):
+def lay_out_kernel(slots_in, out_master, out_first, out_second, slots, sem):
     copies = [
-        pltpu.make_async_copy(a, b, sem.at[i])
-        for i, (a, b) in enumerate(((meta_in, meta), (slots_in, slots), (grad_in, grad)))
+        pltpu.make_async_copy(slots_in.at[pl.ds(a * WIN, WIN)], slots.at[a], sem.at[a]) for a in range(3)
     ]
     for copy in copies:
         copy.start()
-    for copy in copies:
+    for copy, a, out in zip(copies, range(3), (out_master, out_first, out_second)):
         copy.wait()
-    live = slot_ids() < meta[0]
-    delta = meta[1]
-    row = jnp.clip(delta >> 7, 0, GRAD_ROWS - WIN - 1)
-    gradient = jnp.where(live, window(grad, row, delta & 127), 0.0)
-    master, one, two = (slots[a * WIN : (a + 1) * WIN] for a in range(3))
-    first_next = BETA_ONE * one + (1.0 - BETA_ONE) * gradient
-    second_next = BETA_TWO * two + (1.0 - BETA_TWO) * gradient * gradient
-    update = first_next / CORRECT_ONE / (jnp.sqrt(second_next / CORRECT_TWO) + EPSILON)
-    master_next = master - LEARN_RATE * (update + DECAY * master)
-    for value, out in ((master_next, out_master), (first_next, out_first), (second_next, out_second)):
-        value = jnp.where(live, value, 0.0)
+        value = slots[a]
         for t in range(OUT_ROWS):
             wide = min(LANES, NEW_CAP - t * LANES)
             out[:, t * LANES : t * LANES + wide] = value[t : t + 1, :wide]
 
 
 def on_device(features, og, live, former, target, keeper, st0, st1, st2):
-    slots, grad, meta = gather_and_reduce(features, og, live, former, target, keeper, st0, st1, st2)
+    slots = gather_and_reduce(features, og, live, former, target, keeper, st0, st1, st2)
     vm = pl.BlockSpec(memory_space=pltpu.VMEM)
     return pl.pallas_call(
-        update_kernel,
+        lay_out_kernel,
         out_shape=[jax.ShapeDtypeStruct((1, NEW_CAP), jnp.float32)] * 3,
-        in_specs=[pl.BlockSpec(memory_space=pl.ANY)] * 3,
+        in_specs=[pl.BlockSpec(memory_space=pl.ANY)],
         out_specs=[vm] * 3,
         scratch_shapes=[
-            pltpu.SMEM(meta.shape, meta.dtype),
-            pltpu.VMEM(slots.shape, slots.dtype),
-            pltpu.VMEM(grad.shape, grad.dtype),
+            pltpu.VMEM((3, WIN, LANES), jnp.float32),
             pltpu.SemaphoreType.DMA((3,)),
         ],
         compiler_params=pltpu.CompilerParams(vmem_limit_bytes=56 * 1024 * 1024),
-        cost_estimate=pl.CostEstimate(flops=1_000_000, bytes_accessed=1_400_000, transcendentals=0),
-    )(meta, slots, grad)
+        cost_estimate=pl.CostEstimate(flops=100_000, bytes_accessed=320_000, transcendentals=0),
+    )(slots)
 
 
 def solution(mesh):

time: 44.9 us -> 44.7 us (level)
  no operation moved by 1% of the time
where the time goes in v3:
time: 44.7 us; the launch traced here: 44.5 us
  Pallas kernels  43.9 us (98%)
  between operations  0.64 us (1%)
    pallas_call x1, Pallas kernels, gather_and_reduce(): pl.pallas_call(main_kernel, out_shape=jax.ShapeDtypeStruct((3 * WIN, LANE...  42.3 us
    pallas_call x1, Pallas kernels, on_device(): pl.pallas_call(lay_out_kernel, out_shape=[jax.ShapeDtypeStruct((1, NEW_CA...  1.55 us

profile of v3, /device:TPU:1, one launch (start us, length us, event | category | flops | bytes accessed | tf_op | source)
XLA Modules:
  0.0 44.5 jit_solution(8361328788321209541)
XLA Ops:
  0.6 42.3 %shard_map.112.slots_in = f32[312,128]{1,0:T(8,128)} custom-call(s32[64]{0:T(128)} %live_in.1, s32[63]{0:T(128)} %keeper_in.1, s32[64]{0:T(128)} %former_in.1, s32[63]{0:T(128)} %target_in.1, bf16[64,128]{1,0:T(8,128)(2,1)} %feat.1, bf16[512,3584]{1,0:T(8,128)(2,1)} %og.1, f32[1,12544]{1,0:T(1,128)} %st0.1, f32[1,12544]{1,0:T(1,128)} %st1.1, f32[1,12544]{1,0:T(1,128)} %st2.1), custom_call_target="tpu_custom_call" | custom-call | flops 469762048 | bytes 6000000 | tf_op jit(solution)/shard_map/pallas_call | solution.py:335
  42.9 1.6 %shard_map.113 = (f32[1,12659]{1,0:T(1,128)}, f32[1,12659]{1,0:T(1,128)}, f32[1,12659]{1,0:T(1,128)}) custom-call(f32[312,128]{1,0:T(8,128)} %shard_map.112.slots_in), custom_call_target="tpu_custom_call" | custom-call | flops 100000 | bytes 320000 | tf_op jit(solution)/shard_map/pallas_call | solution.py:365

commit v4 on v3

--- a/solution.py
+++ b/solution.py
@@ -33,7 +33,7 @@
 FRONT = 2
 OFFSETS = (-2, -1, 1, 2)
 
-CHUNKS = ((0, 12, "x"), (12, 8, "x"), (20, 8, "y"))
+CHUNKS = ((0, 12, "x"), (12, 8, "y"), (20, 8, "x"))
 
 
 def slot_ids():
@@ -179,13 +179,22 @@
 
     tok = lax.broadcasted_iota(jnp.int32, (TOK, ROWS), 0)
     masked = jnp.where(tok < live_count, feat_all[...].astype(jnp.float32), 0.0).astype(jnp.bfloat16)
-    for w in range(2):
+    def reorder(w):
         mt[w] = lax.dot_general(
             pick[w], masked, (((1,), (1,)), ((), ())), preferred_element_type=jnp.float32
         ).astype(jnp.bfloat16)
 
-    cores = []
-    for k, (j0, nj, order) in enumerate(CHUNKS):
+    reorder(0)
+    reorder(1)
+    def plan(order):
+        if order == "x":
+            return NX, x, at_x, NY, y, at_y
+        return NY, y, at_y, NX, x, at_x
+
+    cores, first = [], []
+
+    def multiply(k):
+        j0, nj, order = CHUNKS[k]
         local[k].wait()
         w = 0 if order == "x" else 1
         for j in range(0, nj, 2):
@@ -204,13 +213,8 @@
             )
         )
 
-    def plan(order):
-        if order == "x":
-            return NX, x, at_x, NY, y, at_y
-        return NY, y, at_y, NX, x, at_x
-
-    first = []
-    for k, (j0, nj, order) in enumerate(CHUNKS):
+    def begin_first(k):
+        j0, nj, order = CHUNKS[k]
         n1, i1, at1, n2, i2, at2 = plan(order)
         g1 = 64 * nj // n1
         half = 64 * nj
@@ -225,6 +229,13 @@
                          s1_s.at[k, o - 1], s1_r.at[k, o - 1], at1(o))
                 )
         first.append(copies)
+
+    multiply(0)
+    multiply(1)
+    begin_first(0)
+    multiply(2)
+    begin_first(1)
+    begin_first(2)
 
     for copy in mine:
         copy.wait()
@@ -285,6 +296,10 @@
             for i, o in enumerate(OFFSETS)
         ])
 
+    early = len(sent) - len(OFFSETS) * n
+    for copy in sent[:early]:
+        copy.wait_send()
+
     for k, (j0, nj, order) in enumerate(CHUNKS):
         for copy in third[k]:
             copy.wait_recv()
@@ -303,7 +318,7 @@
     for a, value in enumerate((master_next, first_next, second_next)):
         slots[a * WIN : (a + 1) * WIN] = jnp.where(live_slot, value, 0.0)
 
-    for copy in sent:
+    for copy in sent[early:]:
         copy.wait_send()
 
 

time: 44.7 us -> 44.4 us (level)
  no operation moved by 1% of the time
where the time goes in v4:
time: 44.4 us; the launch traced here: 44.3 us
  Pallas kernels  43.6 us (98%)
  between operations  0.64 us (1%)
    pallas_call x1, Pallas kernels, gather_and_reduce(): pl.pallas_call(main_kernel, out_shape=jax.ShapeDtypeStruct((3 * WIN, LANE...  42.1 us
    pallas_call x1, Pallas kernels, on_device(): pl.pallas_call(lay_out_kernel, out_shape=[jax.ShapeDtypeStruct((1, NEW_CA...  1.55 us

profile of v4, /device:TPU:1, one launch (start us, length us, event | category | flops | bytes accessed | tf_op | source)
XLA Modules:
  0.0 44.3 jit_solution(4834119763944613167)
XLA Ops:
  0.6 42.1 %shard_map.112.slots_in = f32[312,128]{1,0:T(8,128)} custom-call(s32[64]{0:T(128)} %live_in.1, s32[63]{0:T(128)} %keeper_in.1, s32[64]{0:T(128)} %former_in.1, s32[63]{0:T(128)} %target_in.1, bf16[64,128]{1,0:T(8,128)(2,1)} %feat.1, bf16[512,3584]{1,0:T(8,128)(2,1)} %og.1, f32[1,12544]{1,0:T(1,128)} %st0.1, f32[1,12544]{1,0:T(1,128)} %st1.1, f32[1,12544]{1,0:T(1,128)} %st2.1), custom_call_target="tpu_custom_call" | custom-call | flops 469762048 | bytes 6000000 | tf_op jit(solution)/shard_map/pallas_call | solution.py:350
  42.7 1.6 %shard_map.113 = (f32[1,12659]{1,0:T(1,128)}, f32[1,12659]{1,0:T(1,128)}, f32[1,12659]{1,0:T(1,128)}) custom-call(f32[312,128]{1,0:T(8,128)} %shard_map.112.slots_in), custom_call_target="tpu_custom_call" | custom-call | flops 100000 | bytes 320000 | tf_op jit(solution)/shard_map/pallas_call | solution.py:380

commit v5 on v4

--- a/solution.py
+++ b/solution.py
@@ -290,8 +290,11 @@
         for q in range(n2 - 1):
             total = total + r2[k][q * g2 : (q + 1) * g2]
         fin[k][2 * g2 : 3 * g2] = total
+        cut, most = nj // 8 * 8, (nj + 7) // 8 * 8
+        needed = {2: (cut, g2 - cut), -2: (0, most), 1: (0, g2), -1: (0, g2)}
         third.append([
-            send(fin[k].at[pl.ds(2 * g2, g2)], fin[k].at[pl.ds((2 - o) * g2, g2)],
+            send(fin[k].at[pl.ds(2 * g2 + needed[o][0], needed[o][1])],
+                 fin[k].at[pl.ds((2 - o) * g2 + needed[o][0], needed[o][1])],
                  rd_s.at[k, i], rd_r.at[k, i], at_d(o))
             for i, o in enumerate(OFFSETS)
         ])

time: 44.4 us -> 44.4 us (level)
  no operation moved by 1% of the time
where the time goes in v5:
time: 44.4 us; the launch traced here: 44.3 us
  Pallas kernels  43.6 us (98%)
  between operations  0.64 us (1%)
    pallas_call x1, Pallas kernels, gather_and_reduce(): pl.pallas_call(main_kernel, out_shape=jax.ShapeDtypeStruct((3 * WIN, LANE...  42.1 us
    pallas_call x1, Pallas kernels, on_device(): pl.pallas_call(lay_out_kernel, out_shape=[jax.ShapeDtypeStruct((1, NEW_CA...  1.55 us

profile of v5, /device:TPU:1, one launch (start us, length us, event | category | flops | bytes accessed | tf_op | source)
XLA Modules:
  0.0 44.3 jit_solution(5081788139268807868)
XLA Ops:
  0.6 42.1 %shard_map.112.slots_in = f32[312,128]{1,0:T(8,128)} custom-call(s32[64]{0:T(128)} %live_in.1, s32[63]{0:T(128)} %keeper_in.1, s32[64]{0:T(128)} %former_in.1, s32[63]{0:T(128)} %target_in.1, bf16[64,128]{1,0:T(8,128)(2,1)} %feat.1, bf16[512,3584]{1,0:T(8,128)(2,1)} %og.1, f32[1,12544]{1,0:T(1,128)} %st0.1, f32[1,12544]{1,0:T(1,128)} %st1.1, f32[1,12544]{1,0:T(1,128)} %st2.1), custom_call_target="tpu_custom_call" | custom-call | flops 469762048 | bytes 6000000 | tf_op jit(solution)/shard_map/pallas_call | solution.py:353
  42.7 1.6 %shard_map.113 = (f32[1,12659]{1,0:T(1,128)}, f32[1,12659]{1,0:T(1,128)}, f32[1,12659]{1,0:T(1,128)}) custom-call(f32[312,128]{1,0:T(8,128)} %shard_map.112.slots_in), custom_call_target="tpu_custom_call" | custom-call | flops 100000 | bytes 320000 | tf_op jit(solution)/shard_map/pallas_call | solution.py:383
